TPU v7x, 32 devices: a whole 2x2x4 slice. The times are simulated.
32 devices in a mesh: scen: 2 (over x), rb: 16 (over z, y, core).
Axes of the slice: x: 2, y: 2, z: 4, core: 2. Of those that a mesh axis runs over, the one named last changes fastest.
Arguments:
- right_side: float32 [16384, 32], P(('scen', 'rb')), parts along dimension 0, may hold values from -6 to 6
- blocks: float32 [32, 8, 512, 512], P(('scen', 'rb')), parts along dimension 0, as said below
- block_cols: int32 [32, 8], P(('scen', 'rb')), parts along dimension 0, may hold values from 0 to 15, as said below
- block_counts: int32 [32], P(('scen', 'rb')), parts along dimension 0, may hold values from 1 to 8, as said below
Outputs:
- solution: float32 [16384, 32], P(('scen', 'rb')), parts along dimension 0
- residual: float32 [16384, 32], P(('scen', 'rb')), parts along dimension 0
There are 2 independent parts, one for each index of `scen`. A program takes and returns all parts, laid end to end along the dimension named above; each array names one. Nothing has to cross between parts.
Inputs may be any that keep to these rules, and one draw needn't show every extreme that they name: `block_cols`: slot 0 of row block r holds r. For r >= 1, slots 1 to block_counts[r] - 1 hold distinct column blocks from r + 1 to r + 16, and later slots hold r. Row block 0 links to the whole matrix: its slot 1 holds 8, its slot 2 holds 15, and its slots from 3 on hold column blocks from 1 to 16, distinct among themselves. `block_counts`: row block 0 uses all 8 slots.
All inputs are finite; a program needn't handle non-finite values.
Results may differ from a plain program's by a relative error of at most 0.0003.
Values sent between devices are 32-bit elements; how exact they have to be, the bound alone decides.
A program may use at most 64 MiB of HBM per device.

v0:
```python
import jax
import jax.numpy as jnp
from jax import lax
from jax.sharding import PartitionSpec as P

ITERS = 2


HIGH = lax.Precision.HIGHEST


def solve_spd(matrix, target):
    symmetric = (matrix + matrix.T) * 0.5
    factor = jnp.linalg.cholesky(symmetric)
    middle = lax.linalg.triangular_solve(factor, target, left_side=True, lower=True)
    return lax.linalg.triangular_solve(factor, middle, left_side=True, lower=True, transpose_a=True)


def gram(left, right):
    return jnp.dot(left.T, right, precision=HIGH, preferred_element_type=jnp.float32)


def apply_operator(direction, blocks, block_cols, block_counts):
    width = blocks.shape[2]
    slots = blocks.shape[1]
    columns = direction.shape[1]
    slot_ids = jnp.arange(slots)
    live_mask = (slot_ids < block_counts[0]).astype(jnp.float32)
    mirror_mask = live_mask * (slot_ids >= 1).astype(jnp.float32)
    mirrored = (
        jnp.einsum("sij,ik->sjk", blocks[0], direction, precision=HIGH) * mirror_mask[:, None, None]
    )
    gathered = lax.all_gather(direction, "rb", axis=0, tiled=True)
    total_blocks = gathered.shape[0] // width
    gathered = gathered.reshape(total_blocks, width, columns)
    picked = gathered[block_cols[0]]
    selector = (block_cols[0][:, None] == jnp.arange(total_blocks)[None, :]).astype(jnp.float32)
    spread_terms = jnp.einsum("sn,sjk->njk", selector, mirrored, precision=HIGH).reshape(
        total_blocks * width, columns
    )
    incoming = lax.psum_scatter(spread_terms, "rb", scatter_dimension=0, tiled=True)
    forward = jnp.einsum(
        "sij,sjk->ik", blocks[0], picked * live_mask[:, None, None], precision=HIGH
    )
    return forward + incoming


def body(right_side, blocks, block_cols, block_counts):
    solution = jnp.zeros_like(right_side)
    residual = right_side
    direction = right_side
    norm_now = lax.psum(gram(residual, residual), "rb")
    for step_index in range(ITERS):
        image = apply_operator(direction, blocks, block_cols, block_counts)
        curved = lax.psum(gram(direction, image), "rb")
        alpha = solve_spd(curved, norm_now)
        solution = solution + jnp.dot(
            direction, alpha, precision=HIGH, preferred_element_type=jnp.float32
        )
        residual = residual - jnp.dot(
            image, alpha, precision=HIGH, preferred_element_type=jnp.float32
        )
        if step_index + 1 < ITERS:
            norm_next = lax.psum(gram(residual, residual), "rb")
            beta = solve_spd(norm_now, norm_next)
            direction = residual + jnp.dot(
                direction, beta, precision=HIGH, preferred_element_type=jnp.float32
            )
            norm_now = norm_next
    return (solution, residual)


def solution(mesh):
    in_specs = (
        P(("scen", "rb"), None),
        P(("scen", "rb"), None, None, None),
        P(("scen", "rb"), None),
        P(("scen", "rb")),
    )
    out_specs = (P(("scen", "rb"), None), P(("scen", "rb"), None))
    return jax.shard_map(body, mesh=mesh, in_specs=in_specs, out_specs=out_specs, check_vma=False)
```

profile of v0, /device:TPU:0, one launch (start us, length us, event | category | flops | bytes accessed | tf_op | source)
XLA Modules:
  0.0 431.5 jit_solution(15168056268635658739)
XLA Ops:
  7.2 0.0 copy-start
  7.2 0.0 copy-start.2
  7.2 0.0 all-gather.3.cloned.1.call-start
  7.2 0.7 all-gather.3.cloned.1.call-update
  7.9 0.0 reduce-scatter.3.cloned.1.call-start
  8.6 7.4 %fusion.8 = f32[8,512,32]{1,2,0:T(8,128)S(1)} fusion(f32[1,8,512,512]{3,2,1,0:T(8,128)} %param.10, f32[8]{0:T(128)S(1)} %compare_select_fusion.1, f32[512,32]{0,1:T(8,128)} %param.9), kind=kOutput, calls=%fused_computation.10 | convolution fusion | flops 805437440 | bytes 8978464 | tf_op jit(solution)/shard_map/sij,ik->sjk/dot_general | solution.py:31
  16.1 0.9 fusion.32
  16.9 1.6 copy.35
  18.6 0.0 reduce-scatter.3.cloned.1.call-update
  18.6 0.0 all-gather.5.cloned.1.call-start
  18.7 0.0 copy-done
  18.7 0.2 fusion.67
  18.9 32.0 %all-gather.3.cloned.1.call-done = f32[8192,32]{0,1:T(8,128)} async-done(((f32[512,32]{0,1:T(8,128)}), f32[8192,32]{0,1:T(8,128)}) %all-gather.3.cloned.1.call-update) | async-done | bytes 1048592 | tf_op jit(solution)/shard_map/all_gather | solution.py:33
  50.9 1.3 copy.44
  52.2 0.6 gather_fusion
  52.8 58.0 %reduce-scatter.3.cloned.1.call-done = f32[512,32]{0,1:T(8,128)} async-done(((f32[8192,32]{0,1:T(8,128)}), f32[512,32]{0,1:T(8,128)}) %reduce-scatter.3.cloned.1.call-update) | async-done | bytes 65552 | tf_op jit(solution)/shard_map/reduce_scatter | solution.py:41
  110.9 10.1 %fusion.27 = f32[512,32]{0,1:T(8,128)S(1)} fusion(f32[512,32]{0,1:T(8,128)} %reduce-scatter.3.cloned.1.call-done, f32[1,8,512,512]{3,2,1,0:T(8,128)} %param.10, f32[8,512,32]{1,2,0:T(8,128)S(1)} %gather_fusion, f32[8]{0:T(128)S(1)} %compare_convert_fusion), kind=kOutput, calls=%fused_computation.22 | convolution fusion | flops 805453824 | bytes 9044000 | tf_op jit(solution)/shard_map/sij,sjk->ik/dot_general | solution.py:42
  121.0 0.2 convolution_bitcast_fusion.2
  121.2 57.6 %all-reduce = (f32[32,32]{1,0:T(8,128)S(1)}, f32[32,32]{1,0:T(8,128)S(1)}) all-reduce(f32[32,32]{1,0:T(8,128)S(1)} %fusion.67, f32[32,32]{1,0:T(8,128)S(1)} %convolution_bitcast_fusion.2), channel_id=1, replica_groups=mesh['scen'=2,'rb'=16] {'rb'}, use_global_device_ids=true, to_apply=%region_4.0 | all-reduce | flops 2048 | bytes 16384 | tf_op jit(solution)/shard_map/psum | solution.py:52
  178.8 0.1 copy.26
  178.9 0.1 copy.24
  179.0 0.1 copy.27
  179.0 2.9 cholesky.70
  182.0 0.6 compare_reduce_fusion.1
  182.6 0.7 fusion.41
  183.3 2.4 custom-call.15
  185.7 0.1 copy.25
  185.8 2.9 cholesky.59
  188.8 0.6 compare_reduce_fusion.2
  189.4 0.7 fusion.40
  190.1 2.4 custom-call.13
  192.5 0.2 fusion.55
  192.8 0.1 fusion.57
  192.9 0.3 convolution_subtract_fusion.1
  193.2 0.2 fusion.68
  193.4 57.6 %psum.30 = f32[32,32]{1,0:T(8,128)S(1)} all-reduce(f32[32,32]{1,0:T(8,128)S(1)} %fusion.68), channel_id=1, replica_groups=mesh['scen'=2,'rb'=16] {'rb'}, use_global_device_ids=true, to_apply=%region_5.9 | all-reduce | flops 1024 | bytes 8192 | tf_op jit(solution)/shard_map/psum | solution.py:64
  251.0 0.2 fusion.49
  251.2 0.1 fusion.51
  251.4 0.9 fusion.23
  252.3 0.0 all-gather.5.cloned.1.call-update
  252.3 0.2 reduce-scatter.5.cloned.1.call-start
  252.5 7.2 %fusion.14 = f32[8,512,32]{1,2,0:T(8,128)S(1)} fusion(f32[1,8,512,512]{3,2,1,0:T(8,128)} %param.10, f32[8]{0:T(128)S(1)} %compare_select_fusion.1, f32[512,32]{0,1:T(8,128)} %fusion.23), kind=kOutput, calls=%fused_computation.12 | convolution fusion | flops 805437440 | bytes 8978464 | tf_op jit(solution)/shard_map/sij,ik->sjk/dot_general | solution.py:31
  259.8 0.9 fusion.30
  260.6 1.6 copy.36
  262.3 0.0 reduce-scatter.5.cloned.1.call-update
  262.3 0.3 convolution_bitcast_fusion.1
  262.5 25.2 %all-gather.5.cloned.1.call-done = f32[8192,32]{0,1:T(8,128)} async-done(((f32[512,32]{0,1:T(8,128)}), f32[8192,32]{0,1:T(8,128)}) %all-gather.5.cloned.1.call-update) | async-done | bytes 1048592 | tf_op jit(solution)/shard_map/all_gather | solution.py:33
  287.7 1.3 copy.43
  289.0 0.6 gather_fusion.1
  289.6 58.4 %reduce-scatter.5.cloned.1.call-done = f32[512,32]{0,1:T(8,128)} async-done(((f32[8192,32]{0,1:T(8,128)}), f32[512,32]{0,1:T(8,128)}) %reduce-scatter.5.cloned.1.call-update) | async-done | bytes 65552 | tf_op jit(solution)/shard_map/reduce_scatter | solution.py:41
  348.0 10.1 %fusion.24 = f32[512,32]{0,1:T(8,128)S(1)} fusion(f32[512,32]{0,1:T(8,128)} %reduce-scatter.5.cloned.1.call-done, f32[1,8,512,512]{3,2,1,0:T(8,128)} %param.10, f32[8,512,32]{1,2,0:T(8,128)S(1)} %gather_fusion.1, f32[8]{0:T(128)S(1)} %compare_convert_fusion), kind=kOutput, calls=%fused_computation.21 | convolution fusion | flops 805453824 | bytes 9044000 | tf_op jit(solution)/shard_map/sij,sjk->ik/dot_general | solution.py:42
  358.1 0.0 copy-done.1
  358.1 0.2 fusion.69
  358.3 57.6 %psum.31 = f32[32,32]{1,0:T(8,128)S(1)} all-reduce(f32[32,32]{1,0:T(8,128)S(1)} %fusion.69), channel_id=1, replica_groups=mesh['scen'=2,'rb'=16] {'rb'}, use_global_device_ids=true, to_apply=%region_7.11 | all-reduce | flops 1024 | bytes 8192 | tf_op jit(solution)/shard_map/psum | solution.py:55
  415.9 0.1 copy.30
  416.0 0.1 copy.31
  416.1 2.9 cholesky.81
  419.0 0.6 compare_reduce_fusion
  419.7 0.7 fusion.42
  420.3 2.4 custom-call.17
  422.8 0.2 fusion.43
  423.0 0.1 fusion.45
  423.1 0.9 convolution_subtract_fusion
  424.0 0.9 convolution_add_fusion
  (14 shorter events, 0.2 us)
Async XLA Ops:
  7.2 11.5 %copy-start = (f32[512,32]{0,1:T(8,128)S(1)}, f32[512,32]{0,1:T(8,128)}, u32[]{:S(2)}) copy-start(f32[512,32]{0,1:T(8,128)} %param.9) | copy-start | bytes 196612
  7.2 8.9 %copy-start.2 = (s32[1,8]{1,0:T(1,128)S(1)}, s32[1,8]{1,0:T(1,128)}, u32[]{:S(2)}) copy-start(s32[1,8]{1,0:T(1,128)} %param.11) | copy-start | bytes 100
  7.2 43.7 %all-gather.3.cloned.1.call-start = ((), (), s32[]{:S(2)}) async-start(), calls=%async_computation.2 | async-start | bytes 1114112 | tf_op jit(solution)/shard_map/all_gather | solution.py:33
  7.9 103.0 %reduce-scatter.3.cloned.1.call-start = ((), (), s32[]{:S(2)}) async-start(), calls=%async_computation.3 | async-start | bytes 1114112 | tf_op jit(solution)/shard_map/reduce_scatter | solution.py:41
  18.6 269.1 %all-gather.5.cloned.1.call-start = ((), (), s32[]{:S(2)}) async-start(), calls=%async_computation.4 | async-start | bytes 1114112 | tf_op jit(solution)/shard_map/all_gather | solution.py:33
  252.3 95.7 %reduce-scatter.5.cloned.1.call-start = ((), (), s32[]{:S(2)}) async-start(), calls=%async_computation.5 | async-start | bytes 1114112 | tf_op jit(solution)/shard_map/reduce_scatter | solution.py:41
  262.3 95.8 %copy-start.1 = (f32[512,32]{0,1:T(8,128)S(1)}, f32[512,32]{0,1:T(8,128)}, u32[]{:S(2)}) copy-start(f32[512,32]{0,1:T(8,128)} %fusion.23) | copy-start | bytes 196612
Sparse Core Ops, SparseCore 0:
  10.2 40.6 all-gather.2
  54.5 56.2 reduce-scatter.2
  252.4 35.2 all-gather.4
  291.6 56.3 reduce-scatter.4
where the time goes:
time: 432 us; the launch traced here: 431 us
  waiting for transfers between devices  174 us (40%)
  blocking collectives  173 us (40%)
  matrix products  41.6 us (10%)
  other arithmetic  20.1 us (5%)
  between operations  14.7 us (3%)
  local copies, waits for them, and re-layouts  7.51 us (2%)
    reduce_scatter x2, waiting for transfers between devices, apply_operator(): lax.psum_scatter(spread_terms, 'rb', scatter_dimension=0, tiled=True)  116 us
    psum x1, blocking collectives, body(): norm_now = lax.psum(gram(residual, residual), 'rb')  57.6 us
    psum x1, blocking collectives, body(): norm_next = lax.psum(gram(residual, residual), 'rb')  57.6 us
    psum x1, blocking collectives, body(): curved = lax.psum(gram(direction, image), 'rb')  57.6 us
    all_gather x2, waiting for transfers between devices, apply_operator(): gathered = lax.all_gather(direction, 'rb', axis=0, tiled=True)  57.2 us
    dot_general x2, matrix products, apply_operator(): jnp.einsum('sij,sjk->ik', blocks[0], picked * live_mask[:, None, None], p...  20.1 us
    dot_general x2, matrix products, apply_operator(): jnp.einsum('sij,ik->sjk', blocks[0], direction, precision=HIGH)  14.7 us
    another operation x9, other arithmetic, solve_spd(): factor = jnp.linalg.cholesky(symmetric)  10.8 us
  transfers between devices with their start and end apart: 4, of which 4 were waited for; matrix products, arithmetic and copies ran while one was open for 6% of the time, Pallas kernels for 0%

commit v1 on v0

v1 whole, which is shorter than its diff:
```python
import functools

import jax
import jax.numpy as jnp
from jax import lax
from jax.experimental import pallas as pl
from jax.experimental.pallas import tpu as pltpu
from jax.sharding import PartitionSpec as P

F32 = jnp.float32
BF16 = jnp.bfloat16
HIGH = lax.Precision.HIGHEST
NN = (((1,), (0,)), ((), ()))
NT = (((1,), (1,)), ((), ()))


def exact(a, b, dims=NN):
    return lax.dot_general(a, b, dims, precision=HIGH, preferred_element_type=F32)


def fast(a, b, dims):
    return lax.dot_general(a, b, dims, preferred_element_type=F32)


def halves(x):
    hi = x.astype(BF16)
    return hi, (x - hi.astype(F32)).astype(BF16)


def stacked(x):
    hi, lo = halves(x)
    return jnp.concatenate([hi, lo], axis=0)


def pack(g):
    return jnp.concatenate([g[8 * i : 8 * i + 8] for i in range(g.shape[0] // 8)], axis=1)


def unpack(p):
    nr = p.shape[1] // 4
    return jnp.concatenate([p[:, nr * i : nr * i + nr] for i in range(4)], axis=0)


def solve_t(matrix, target):
    n = matrix.shape[0]
    work = jnp.concatenate([(matrix + matrix.T) * 0.5, target], axis=1)
    rows = lax.broadcasted_iota(jnp.int32, work.shape, 0)
    for k in range(n):
        pivot_row = work[k : k + 1, :] / work[k : k + 1, k : k + 1]
        work = jnp.where(rows == k, pivot_row, work - work[:, k : k + 1] * pivot_row)
    return work[:, n:].T


def loop(lo, hi, step):
    if hi - lo <= 4:
        for i in range(lo, hi):
            step(i)
    else:
        lax.fori_loop(lo, hi, lambda i, c: (step(i), c)[1], 0)


def kernel(
    n, ny, cols_ref, count_ref, rhs_ref, blocks_ref, out_ref,
    stage, bh, bl, gat, mir, cs, cr, ys, yr, zs, zr, acc, gp, gz,
    load_sem, gzs, gzr, gys, gyr, gcs, gcr, rcs, rcr, rys, ryr, rzs, rzr, pps, ppr, pzs, pzr,
):
    slots = blocks_ref.shape[1]
    nz = n // (2 * ny)
    plane = 2 * ny
    me = lax.axis_index("rb")
    c = lax.rem(me, 2)
    y = lax.rem(me // 2, ny)
    z = me // plane
    here = lax.rem(me, plane)

    def bid(zz, yy, cc):
        return (zz * ny + yy) * 2 + cc

    def remote(src, dst, ss, rs, dev):
        return pltpu.make_async_remote_copy(
            src_ref=src, dst_ref=dst, send_sem=ss, recv_sem=rs,
            device_id={"rb": dev}, device_id_type=pl.DeviceIdType.MESH,
        )

    def load(s):
        return pltpu.make_async_copy(blocks_ref.at[0, s], stage.at[s], load_sem.at[s])

    loop(0, slots, lambda s: load(s).start())

    barrier = pltpu.get_barrier_semaphore()

    def greet(dev):
        pl.semaphore_signal(
            barrier, inc=1, device_id={"rb": dev}, device_id_type=pl.DeviceIdType.MESH
        )

    def plane_dev(k):
        return z * plane + lax.rem(here + k, plane)

    def line_dev(k):
        return lax.rem(z + k, nz) * plane + here

    loop(1, plane, lambda k: greet(plane_dev(k)))
    loop(1, nz, lambda k: greet(line_dev(k)))

    rhs = rhs_ref[...]
    zero = jnp.zeros_like(rhs)
    for it in range(2):
        gat[it, n] = zero
    gat[0, me] = rhs
    mir[0] = zero
    pl.semaphore_wait(barrier, plane - 1 + nz - 1)

    def copy_gz(it, dz, block, dev):
        ref = gat.at[it, block]
        return remote(ref, ref, gzs.at[it, dz], gzr.at[it, dz], dev)

    def send_gz(it, dz):
        return copy_gz(it, dz, me, me - dz * plane)

    def recv_gz(it, dz):
        return copy_gz(it, dz, me + dz * plane, me)

    def copy_gy(it, dz, block):
        ref = gat.at[it, block]
        return remote(ref, ref, gys.at[it, dz], gyr.at[it, dz], bid(z, 1 - y, c))

    def copy_gc(it, dz, j, block):
        ref = gat.at[it, block]
        return remote(
            ref, ref, gcs.at[it, j * nz + dz], gcr.at[it, j * nz + dz], bid(z, y, 1 - c)
        )

    def other(yy, j):
        return yy if j == 0 else 1 - yy

    def gather_start(it):
        def step(dz):
            @pl.when(z >= dz)
            def _():
                send_gz(it, dz).start()

        loop(1, nz, step)
        if ny == 2:
            copy_gy(it, 0, me).start()
        copy_gc(it, 0, 0, me).start()

    def gather_relay_z(it):
        def step(dz):
            @pl.when(z + dz < nz)
            def _():
                recv_gz(it, dz).wait_recv()
                block = me + dz * plane
                if ny == 2:
                    copy_gy(it, dz, block).start()
                copy_gc(it, dz, 0, block).start()

        loop(1, nz, step)

    def gather_relay_y(it):
        if ny == 1:
            return

        def step(dz):
            @pl.when(z + dz < nz)
            def _():
                block = bid(z + dz, 1 - y, c)
                copy_gy(it, dz, block).wait_recv()
                copy_gc(it, dz, 1, block).start()

        loop(0, nz, step)

    def gather_finish(it):
        def step(dz):
            @pl.when(z + dz < nz)
            def _():
                for j in range(ny):
                    copy_gc(it, dz, j, bid(z + dz, other(y, j), 1 - c)).wait_recv()

        loop(0, nz, step)

    def gather_drain(it):
        def step_z(dz):
            @pl.when(z >= dz)
            def _():
                send_gz(it, dz).wait_send()

        loop(1, nz, step_z)

        def step(dz):
            @pl.when(z + dz < nz)
            def _():
                if ny == 2:
                    copy_gy(it, dz, bid(z + dz, y, c)).wait_send()
                for j in range(ny):
                    copy_gc(it, dz, j, bid(z + dz, other(y, j), c)).wait_send()

        loop(0, nz, step)

    count = count_ref[0]
    cols = [cols_ref[0, s] for s in range(slots)]
    live = [jnp.int32(s) < count for s in range(slots)]

    def spread(target):
        first = jnp.int32(0)
        for s in (1, 2):
            first = jnp.where(live[s] & (cols[s] == target), s, first)
        second = jnp.int32(0)
        for s in range(3, slots):
            second = jnp.where(live[s] & (cols[s] == target), s, second)
        return mir[first] + mir[second]

    def copy_rc(it, dz):
        return remote(
            cs.at[it, dz], cr.at[it, dz], rcs.at[it, dz], rcr.at[it, dz], bid(z, y, 1 - c)
        )

    def copy_ry(it, dz):
        return remote(
            ys.at[it, dz], yr.at[it, dz], rys.at[it, dz], ryr.at[it, dz], bid(z, 1 - y, c)
        )

    def copy_rz(it, dz, dev):
        return remote(zs.at[it, dz], zr.at[it, dz], rzs.at[it, dz], rzr.at[it, dz], dev)

    def far_first(step):
        loop(1, nz, step)
        step(0)

    def reduce_core(it):
        def step(dz):
            @pl.when(z + dz < nz)
            def _():
                for yy in range(ny):
                    cs[it, dz, yy] = spread(bid(z + dz, yy, 1 - c))
                copy_rc(it, dz).start()

        far_first(step)

    def reduce_y(it):
        def step(dz):
            @pl.when(z + dz < nz)
            def _():
                copy_rc(it, dz).wait_recv()
                if ny == 2:
                    ys[it, dz] = spread(bid(z + dz, 1 - y, c)) + cr[it, dz, 1 - y]
                    copy_ry(it, dz).start()

        far_first(step)

    def reduce_z(it):
        def part(dz):
            mine = spread(bid(z + dz, y, c)) + cr[it, dz, y]
            if ny == 2:
                copy_ry(it, dz).wait_recv()
                mine = mine + yr[it, dz]
            return mine

        def step(dz):
            @pl.when(z + dz < nz)
            def _():
                zs[it, dz] = part(dz)
                copy_rz(it, dz, me + dz * plane).start()

        loop(1, nz, step)
        acc[...] = part(0)

    def reduce_finish(it):
        def step(dz):
            @pl.when(z >= dz)
            def _():
                copy_rz(it, dz, me).wait_recv()
                acc[...] += zr[it, dz]

        loop(1, nz, step)
        return acc[...]

    def reduce_drain(it):
        def step(dz):
            @pl.when(z + dz < nz)
            def _():
                copy_rc(it, dz).wait_send()
                if ny == 2:
                    copy_ry(it, dz).wait_send()

        loop(0, nz, step)

        def step_z(dz):
            @pl.when(z + dz < nz)
            def _():
                copy_rz(it, dz, me).wait_send()

        loop(1, nz, step_z)

    def copy_pp(i, k, slot, dev):
        ref = gp.at[i, slot]
        return remote(ref, ref, pps.at[i, k], ppr.at[i, k], dev)

    def copy_pz(i, k, slot, dev):
        ref = gz.at[i, slot]
        return remote(ref, ref, pzs.at[i, k], pzr.at[i, k], dev)

    def sum_start(i, value):
        gp[i, here] = value
        loop(1, plane, lambda k: copy_pp(i, k, here, plane_dev(k)).start())

    def sum_middle(i):
        loop(
            1, plane,
            lambda k: copy_pp(i, k, lax.rem(here - k + plane, plane), plane_dev(k)).wait_recv(),
        )
        total = gp[i, 0]
        for k in range(1, plane):
            total = total + gp[i, k]
        gz[i, z] = total
        loop(1, nz, lambda k: copy_pz(i, k, z, line_dev(k)).start())

    def sum_finish(i):
        loop(
            1, nz,
            lambda k: copy_pz(i, k, lax.rem(z - k + nz, nz), line_dev(k)).wait_recv(),
        )
        total = gz[i, 0]
        for k in range(1, nz):
            total = total + gz[i, k]
        return total

    def sum_drain(i):
        loop(1, plane, lambda k: copy_pp(i, k, here, plane_dev(k)).wait_send())
        loop(1, nz, lambda k: copy_pz(i, k, z, line_dev(k)).wait_send())

    nr = rhs.shape[0]

    def product(x2, s, dims):
        both = fast(x2, bh[s], dims)
        return both[:nr] + both[nr:] + fast(x2[:nr], bl[s], dims)

    def split_block(s):
        load(s).wait()
        hi, lo = halves(stage[s])
        bh[s] = hi
        bl[s] = lo

    def mirror(x2, lo, hi):
        def step(s, carry):
            mir[s] = product(x2, s, NN)
            return carry

        lax.fori_loop(lo, hi, step, 0)

    def forward(it):
        def step(s, total):
            col = jnp.where(s < count, cols_ref[0, s], n)
            return total + product(stacked(gat[it, col]), s, NT)

        return lax.fori_loop(1, slots, step, zero)

    def operator(it, x, first):
        x2 = stacked(x)

        if first:
            def step(s, carry):
                split_block(s)
                mir[s] = product(x2, s, NN)
                return carry

            lax.fori_loop(1, slots // 2, step, 0)
            gather_relay_z(it)
            lax.fori_loop(slots // 2, slots, step, 0)
            split_block(0)
        else:
            mirror(x2, 1, slots // 2)
            gather_relay_z(it)
            mirror(x2, slots // 2, slots)
        reduce_core(it)
        gather_relay_y(it)
        reduce_y(it)
        own = product(x2, 0, NT)
        gather_finish(it)
        return own

    packed_zero = jnp.zeros((8, 4 * nr), F32)

    gather_start(0)
    own0 = operator(0, rhs, True)
    fwd0 = forward(0)
    curved = exact(rhs, own0 + fwd0, NT) + exact(fwd0, rhs, NT)
    sum_start(0, jnp.concatenate([pack(curved), pack(exact(rhs, rhs, NT))], axis=0))
    reduce_z(0)
    sum_middle(0)
    sums = sum_finish(0)
    norm0 = unpack(sums[8:])
    alpha = solve_t(unpack(sums[:8]), norm0)
    image0 = own0 + fwd0 + reduce_finish(0)
    residual = rhs - exact(alpha, image0)
    gat[1, me] = residual
    gather_start(1)
    sum_start(1, jnp.concatenate([pack(exact(residual, residual, NT)), packed_zero], axis=0))
    solution_t = exact(alpha, rhs)

    sum_middle(1)
    own1 = operator(1, residual, False)
    norm1 = unpack(sum_finish(1)[:8])
    beta = solve_t(norm0, norm1)
    fwd1 = forward(1)
    direction = residual + exact(beta, rhs)
    fwd_d = fwd1 + exact(beta, fwd0)
    own_d = own1 + exact(beta, own0)
    curved = exact(direction, own_d + fwd_d, NT) + exact(fwd_d, direction, NT)
    sum_start(2, jnp.concatenate([pack(curved), packed_zero], axis=0))
    reduce_z(1)
    sum_middle(2)
    alpha = solve_t(unpack(sum_finish(2)[:8]), norm1)
    image = own1 + fwd1 + reduce_finish(1) + exact(beta, image0)
    out_ref[0] = solution_t + exact(alpha, direction)
    out_ref[1] = residual - exact(alpha, image)

    for it in range(2):
        gather_drain(it)
        reduce_drain(it)
    for i in range(3):
        sum_drain(i)


def body(n, ny, right_side, blocks, block_cols, block_counts):
    width, nr = right_side.shape
    slots = blocks.shape[1]
    nz = n // (2 * ny)
    dma = pltpu.SemaphoreType.DMA
    vec = (nr, width)
    out = pl.pallas_call(
        functools.partial(kernel, n, ny),
        out_shape=jax.ShapeDtypeStruct((2,) + vec, F32),
        in_specs=[
            pl.BlockSpec(memory_space=pltpu.SMEM),
            pl.BlockSpec(memory_space=pltpu.SMEM),
            pl.BlockSpec(memory_space=pltpu.VMEM),
            pl.BlockSpec(memory_space=pl.ANY),
        ],
        out_specs=pl.BlockSpec(memory_space=pltpu.VMEM),
        scratch_shapes=[
            pltpu.VMEM((slots, width, width), F32),
            pltpu.VMEM((slots, width, width), BF16),
            pltpu.VMEM((slots, width, width), BF16),
            pltpu.VMEM((2, n + 1) + vec, F32),
            pltpu.VMEM((slots,) + vec, F32),
            pltpu.VMEM((2, nz, ny) + vec, F32),
            pltpu.VMEM((2, nz, ny) + vec, F32),
            pltpu.VMEM((2, nz if ny == 2 else 1) + vec, F32),
            pltpu.VMEM((2, nz if ny == 2 else 1) + vec, F32),
            pltpu.VMEM((2, nz) + vec, F32),
            pltpu.VMEM((2, nz) + vec, F32),
            pltpu.VMEM(vec, F32),
            pltpu.VMEM((3, 2 * ny, 16, 4 * nr), F32),
            pltpu.VMEM((3, nz, 16, 4 * nr), F32),
            dma((slots,)),
            dma((2, nz)), dma((2, nz)),
            dma((2, nz if ny == 2 else 1)), dma((2, nz if ny == 2 else 1)),
            dma((2, nz * ny)), dma((2, nz * ny)),
            dma((2, nz)), dma((2, nz)),
            dma((2, nz if ny == 2 else 1)), dma((2, nz if ny == 2 else 1)),
            dma((2, nz)), dma((2, nz)),
            dma((3, 2 * ny)), dma((3, 2 * ny)),
            dma((3, nz)), dma((3, nz)),
        ],
        compiler_params=pltpu.CompilerParams(
            collective_id=0, has_side_effects=True, vmem_limit_bytes=58 * 2**20
        ),
    )(block_cols, block_counts, right_side.T, blocks)
    return out[0].T, out[1].T


def solution(mesh):
    in_specs = (
        P(("scen", "rb"), None),
        P(("scen", "rb"), None, None, None),
        P(("scen", "rb"), None),
        P(("scen", "rb")),
    )
    out_specs = (P(("scen", "rb"), None), P(("scen", "rb"), None))
    ny = max(1, 4 // mesh.shape["scen"])
    step = functools.partial(body, mesh.shape["rb"], ny)
    return jax.shard_map(step, mesh=mesh, in_specs=in_specs, out_specs=out_specs, check_vma=False)
```

time: 432 us -> 64.8 us (0.15)
  the two profiles are of different devices: /device:TPU:0 before, /device:TPU:25 now
where the time goes in v1:
time: 64.8 us; the launch traced here: 64.6 us
  Pallas kernels  61.8 us (95%)
  local copies, waits for them, and re-layouts  1.53 us (2%)
  between operations  1.29 us (2%)
    pallas_call x1, Pallas kernels, body(): pl.pallas_call(functools.partial(kernel, n, ny), out_shape=jax.ShapeDtype...  61.8 us
    transpose x1, local copies, waits for them, and re-layouts, body(): return (out[0].T, out[1].T)  1.53 us

profile of v1, /device:TPU:25, one launch (start us, length us, event | category | flops | bytes accessed | tf_op | source)
XLA Modules:
  0.0 64.6 jit_solution(17054629218772733135)
XLA Ops:
  1.3 61.8 %shard_map.59 = f32[2,32,512]{2,1,0:T(8,128)} custom-call(s32[1,8]{1,0:T(1,128)} %cols_ref.1, s32[1]{0:T(128)S(6)} %copy.6.count_ref, f32[32,512]{1,0:T(8,128)} %bitcast.9, f32[1,8,512,512]{3,2,1,0:T(8,128)} %blocks_ref.1), custom_call_target="tpu_custom_call" | custom-call | tf_op jit(solution)/shard_map/pallas_call | solution.py:431
  63.1 1.5 %slice_bitcast_fusion = (f32[512,32]{0,1:T(8,128)}, f32[512,32]{0,1:T(8,128)}) fusion(f32[2,32,512]{2,1,0:T(8,128)} %shard_map.59), kind=kLoop, calls=%fused_computation | loop fusion | bytes 262144 | tf_op jit(solution)/shard_map/transpose | solution.py:470

commit v2 on v1

--- a/solution.py
+++ b/solution.py
@@ -45,14 +45,34 @@
     n = matrix.shape[0]
     work = jnp.concatenate([(matrix + matrix.T) * 0.5, target], axis=1)
     rows = lax.broadcasted_iota(jnp.int32, work.shape, 0)
-    for k in range(n):
-        pivot_row = work[k : k + 1, :] / work[k : k + 1, k : k + 1]
-        work = jnp.where(rows == k, pivot_row, work - work[:, k : k + 1] * pivot_row)
+    wide = (1, work.shape[1])
+    for k in range(0, n, 4):
+        span = range(4)
+        row = [work[k + i : k + i + 1, :] for i in span]
+        entry = [
+            [jnp.broadcast_to(row[i][:, k + j : k + j + 1], wide) for j in span] for i in span
+        ]
+        for p in span:
+            inverse = 1.0 / entry[p][p]
+            row[p] = row[p] * inverse
+            for j in range(p + 1, 4):
+                entry[p][j] = entry[p][j] * inverse
+            for i in span:
+                if i != p:
+                    row[i] = row[i] - entry[i][p] * row[p]
+                    for j in range(p + 1, 4):
+                        entry[i][j] = entry[i][j] - entry[i][p] * entry[p][j]
+        swept = work
+        for p in span:
+            swept = swept - work[:, k + p : k + p + 1] * row[p]
+        for p in span:
+            swept = jnp.where(rows == k + p, row[p], swept)
+        work = swept
     return work[:, n:].T
 
 
 def loop(lo, hi, step):
-    if hi - lo <= 4:
+    if hi - lo <= 16:
         for i in range(lo, hi):
             step(i)
     else:
@@ -61,8 +81,8 @@
 
 def kernel(
     n, ny, cols_ref, count_ref, rhs_ref, blocks_ref, out_ref,
-    stage, bh, bl, gat, mir, cs, cr, ys, yr, zs, zr, acc, gp, gz,
-    load_sem, gzs, gzr, gys, gyr, gcs, gcr, rcs, rcr, rys, ryr, rzs, rzr, pps, ppr, pzs, pzr,
+    stage, bh, bl, gat, mir, cs, cr, ys, yr, zs, zr, acc, gp,
+    load_sem, gzs, gzr, gys, gyr, gcs, gcr, rcs, rcr, rys, ryr, rzs, rzr, pps, ppr,
 ):
     slots = blocks_ref.shape[1]
     nz = n // (2 * ny)
@@ -71,7 +91,6 @@
     c = lax.rem(me, 2)
     y = lax.rem(me // 2, ny)
     z = me // plane
-    here = lax.rem(me, plane)
 
     def bid(zz, yy, cc):
         return (zz * ny + yy) * 2 + cc
@@ -85,23 +104,18 @@
     def load(s):
         return pltpu.make_async_copy(blocks_ref.at[0, s], stage.at[s], load_sem.at[s])
 
+    barrier = pltpu.get_barrier_semaphore()
+
+    def peer(k):
+        return lax.rem(me + k, n)
+
+    def greet(k):
+        pl.semaphore_signal(
+            barrier, inc=1, device_id={"rb": peer(k)}, device_id_type=pl.DeviceIdType.MESH
+        )
+
+    loop(1, n, greet)
     loop(0, slots, lambda s: load(s).start())
-
-    barrier = pltpu.get_barrier_semaphore()
-
-    def greet(dev):
-        pl.semaphore_signal(
-            barrier, inc=1, device_id={"rb": dev}, device_id_type=pl.DeviceIdType.MESH
-        )
-
-    def plane_dev(k):
-        return z * plane + lax.rem(here + k, plane)
-
-    def line_dev(k):
-        return lax.rem(z + k, nz) * plane + here
-
-    loop(1, plane, lambda k: greet(plane_dev(k)))
-    loop(1, nz, lambda k: greet(line_dev(k)))
 
     rhs = rhs_ref[...]
     zero = jnp.zeros_like(rhs)
@@ -109,7 +123,6 @@
         gat[it, n] = zero
     gat[0, me] = rhs
     mir[0] = zero
-    pl.semaphore_wait(barrier, plane - 1 + nz - 1)
 
     def copy_gz(it, dz, block, dev):
         ref = gat.at[it, block]
@@ -296,38 +309,16 @@
         ref = gp.at[i, slot]
         return remote(ref, ref, pps.at[i, k], ppr.at[i, k], dev)
 
-    def copy_pz(i, k, slot, dev):
-        ref = gz.at[i, slot]
-        return remote(ref, ref, pzs.at[i, k], pzr.at[i, k], dev)
-
     def sum_start(i, value):
-        gp[i, here] = value
-        loop(1, plane, lambda k: copy_pp(i, k, here, plane_dev(k)).start())
-
-    def sum_middle(i):
-        loop(
-            1, plane,
-            lambda k: copy_pp(i, k, lax.rem(here - k + plane, plane), plane_dev(k)).wait_recv(),
-        )
-        total = gp[i, 0]
-        for k in range(1, plane):
-            total = total + gp[i, k]
-        gz[i, z] = total
-        loop(1, nz, lambda k: copy_pz(i, k, z, line_dev(k)).start())
+        gp[i, me] = pack(value)
+        loop(1, n, lambda k: copy_pp(i, k, me, peer(k)).start())
 
     def sum_finish(i):
-        loop(
-            1, nz,
-            lambda k: copy_pz(i, k, lax.rem(z - k + nz, nz), line_dev(k)).wait_recv(),
-        )
-        total = gz[i, 0]
-        for k in range(1, nz):
-            total = total + gz[i, k]
-        return total
+        loop(1, n, lambda k: copy_pp(i, k, lax.rem(me - k + n, n), peer(k)).wait_recv())
+        return unpack(jnp.sum(gp[i], axis=0))
 
     def sum_drain(i):
-        loop(1, plane, lambda k: copy_pp(i, k, here, plane_dev(k)).wait_send())
-        loop(1, nz, lambda k: copy_pz(i, k, z, line_dev(k)).wait_send())
+        loop(1, n, lambda k: copy_pp(i, k, me, peer(k)).wait_send())
 
     nr = rhs.shape[0]
 
@@ -355,70 +346,66 @@
 
         return lax.fori_loop(1, slots, step, zero)
 
-    def operator(it, x, first):
-        x2 = stacked(x)
-
-        if first:
-            def step(s, carry):
-                split_block(s)
-                mir[s] = product(x2, s, NN)
-                return carry
-
-            lax.fori_loop(1, slots // 2, step, 0)
-            gather_relay_z(it)
-            lax.fori_loop(slots // 2, slots, step, 0)
-            split_block(0)
-        else:
-            mirror(x2, 1, slots // 2)
-            gather_relay_z(it)
-            mirror(x2, slots // 2, slots)
-        reduce_core(it)
-        gather_relay_y(it)
-        reduce_y(it)
-        own = product(x2, 0, NT)
-        gather_finish(it)
-        return own
-
-    packed_zero = jnp.zeros((8, 4 * nr), F32)
-
+    norm_part = exact(rhs, rhs, NT)
+    pair = stacked(rhs)
+    pl.semaphore_wait(barrier, n - 1)
     gather_start(0)
-    own0 = operator(0, rhs, True)
+    sum_start(0, norm_part)
+
+    def split_mirror(s, carry):
+        split_block(s)
+        mir[s] = product(pair, s, NN)
+        return carry
+
+    lax.fori_loop(1, slots // 2, split_mirror, 0)
+    gather_relay_z(0)
+    lax.fori_loop(slots // 2, slots, split_mirror, 0)
+    split_block(0)
+    own0 = product(pair, 0, NT)
+    gather_relay_y(0)
+    reduce_core(0)
+    reduce_y(0)
+    gather_finish(0)
     fwd0 = forward(0)
-    curved = exact(rhs, own0 + fwd0, NT) + exact(fwd0, rhs, NT)
-    sum_start(0, jnp.concatenate([pack(curved), pack(exact(rhs, rhs, NT))], axis=0))
+    sum_start(1, exact(rhs, own0 + fwd0, NT) + exact(fwd0, rhs, NT))
     reduce_z(0)
-    sum_middle(0)
-    sums = sum_finish(0)
-    norm0 = unpack(sums[8:])
-    alpha = solve_t(unpack(sums[:8]), norm0)
+    norm0 = sum_finish(0)
+    alpha = solve_t(sum_finish(1), norm0)
     image0 = own0 + fwd0 + reduce_finish(0)
     residual = rhs - exact(alpha, image0)
     gat[1, me] = residual
     gather_start(1)
-    sum_start(1, jnp.concatenate([pack(exact(residual, residual, NT)), packed_zero], axis=0))
+    sum_start(2, exact(residual, residual, NT))
     solution_t = exact(alpha, rhs)
 
-    sum_middle(1)
-    own1 = operator(1, residual, False)
-    norm1 = unpack(sum_finish(1)[:8])
+    pair = stacked(residual)
+    mirror(pair, 1, slots // 2)
+    gather_relay_z(1)
+    mirror(pair, slots // 2, slots)
+    own1 = product(pair, 0, NT)
+    norm1 = sum_finish(2)
     beta = solve_t(norm0, norm1)
+    gather_relay_y(1)
+    reduce_core(1)
+    reduce_y(1)
+    direction = residual + exact(beta, rhs)
+    own_d = own1 + exact(beta, own0)
+    turned0 = exact(beta, fwd0)
+    image_d = own1 + exact(beta, image0)
+    gather_finish(1)
     fwd1 = forward(1)
-    direction = residual + exact(beta, rhs)
-    fwd_d = fwd1 + exact(beta, fwd0)
-    own_d = own1 + exact(beta, own0)
-    curved = exact(direction, own_d + fwd_d, NT) + exact(fwd_d, direction, NT)
-    sum_start(2, jnp.concatenate([pack(curved), packed_zero], axis=0))
+    fwd_d = fwd1 + turned0
+    sum_start(3, exact(direction, own_d + fwd_d, NT) + exact(fwd_d, direction, NT))
     reduce_z(1)
-    sum_middle(2)
-    alpha = solve_t(unpack(sum_finish(2)[:8]), norm1)
-    image = own1 + fwd1 + reduce_finish(1) + exact(beta, image0)
+    alpha = solve_t(sum_finish(3), norm1)
+    image = image_d + fwd1 + reduce_finish(1)
     out_ref[0] = solution_t + exact(alpha, direction)
     out_ref[1] = residual - exact(alpha, image)
 
     for it in range(2):
         gather_drain(it)
         reduce_drain(it)
-    for i in range(3):
+    for i in range(4):
         sum_drain(i)
 
 
@@ -451,8 +438,7 @@
             pltpu.VMEM((2, nz) + vec, F32),
             pltpu.VMEM((2, nz) + vec, F32),
             pltpu.VMEM(vec, F32),
-            pltpu.VMEM((3, 2 * ny, 16, 4 * nr), F32),
-            pltpu.VMEM((3, nz, 16, 4 * nr), F32),
+            pltpu.VMEM((4, n, 8, 4 * nr), F32),
             dma((slots,)),
             dma((2, nz)), dma((2, nz)),
             dma((2, nz if ny == 2 else 1)), dma((2, nz if ny == 2 else 1)),
@@ -460,8 +446,7 @@
             dma((2, nz)), dma((2, nz)),
             dma((2, nz if ny == 2 else 1)), dma((2, nz if ny == 2 else 1)),
             dma((2, nz)), dma((2, nz)),
-            dma((3, 2 * ny)), dma((3, 2 * ny)),
-            dma((3, nz)), dma((3, nz)),
+            dma((4, n)), dma((4, n)),
         ],
         compiler_params=pltpu.CompilerParams(
             collective_id=0, has_side_effects=True, vmem_limit_bytes=58 * 2**20

time: 64.8 us -> 59.6 us (0.920)
  the two profiles are of different devices: /device:TPU:25 before, /device:TPU:0 now
where the time goes in v2:
time: 59.6 us; the launch traced here: 59.4 us
  Pallas kernels  56.6 us (95%)
  local copies, waits for them, and re-layouts  1.53 us (3%)
  between operations  1.29 us (2%)
    pallas_call x1, Pallas kernels, body(): pl.pallas_call(functools.partial(kernel, n, ny), out_shape=jax.ShapeDtype...  56.6 us
    transpose x1, local copies, waits for them, and re-layouts, body(): return (out[0].T, out[1].T)  1.53 us

profile of v2, /device:TPU:0, one launch (start us, length us, event | category | flops | bytes accessed | tf_op | source)
XLA Modules:
  0.0 59.4 jit_solution(15500839191654016197)
XLA Ops:
  1.3 56.6 %shard_map.59 = f32[2,32,512]{2,1,0:T(8,128)} custom-call(s32[1,8]{1,0:T(1,128)} %cols_ref.1, s32[1]{0:T(128)S(6)} %copy.6.count_ref, f32[32,512]{1,0:T(8,128)} %bitcast.9, f32[1,8,512,512]{3,2,1,0:T(8,128)} %blocks_ref.1), custom_call_target="tpu_custom_call" | custom-call | tf_op jit(solution)/shard_map/pallas_call | solution.py:418
  57.8 1.5 %slice_bitcast_fusion = (f32[512,32]{0,1:T(8,128)}, f32[512,32]{0,1:T(8,128)}) fusion(f32[2,32,512]{2,1,0:T(8,128)} %shard_map.59), kind=kLoop, calls=%fused_computation | loop fusion | bytes 262144 | tf_op jit(solution)/shard_map/transpose | solution.py:455

commit v3 on v2

--- a/solution.py
+++ b/solution.py
@@ -153,22 +153,19 @@
             def _():
                 send_gz(it, dz).start()
 
-        loop(1, nz, step)
+        loop(1, nz, lambda k: step(nz - k))
         if ny == 2:
             copy_gy(it, 0, me).start()
         copy_gc(it, 0, 0, me).start()
 
-    def gather_relay_z(it):
-        def step(dz):
-            @pl.when(z + dz < nz)
-            def _():
-                recv_gz(it, dz).wait_recv()
-                block = me + dz * plane
-                if ny == 2:
-                    copy_gy(it, dz, block).start()
-                copy_gc(it, dz, 0, block).start()
-
-        loop(1, nz, step)
+    def gather_relay_z(it, dz):
+        @pl.when(z + dz < nz)
+        def _():
+            recv_gz(it, dz).wait_recv()
+            block = me + dz * plane
+            if ny == 2:
+                copy_gy(it, dz, block).start()
+            copy_gc(it, dz, 0, block).start()
 
     def gather_relay_y(it):
         if ny == 1:
@@ -357,9 +354,12 @@
         mir[s] = product(pair, s, NN)
         return carry
 
-    lax.fori_loop(1, slots // 2, split_mirror, 0)
-    gather_relay_z(0)
-    lax.fori_loop(slots // 2, slots, split_mirror, 0)
+    lax.fori_loop(1, 4, split_mirror, 0)
+    gather_relay_z(0, 1)
+    lax.fori_loop(4, 6, split_mirror, 0)
+    gather_relay_z(0, 2)
+    lax.fori_loop(6, slots, split_mirror, 0)
+    loop(3, nz, lambda dz: gather_relay_z(0, dz))
     split_block(0)
     own0 = product(pair, 0, NT)
     gather_relay_y(0)
@@ -379,9 +379,12 @@
     solution_t = exact(alpha, rhs)
 
     pair = stacked(residual)
-    mirror(pair, 1, slots // 2)
-    gather_relay_z(1)
-    mirror(pair, slots // 2, slots)
+    mirror(pair, 1, 4)
+    gather_relay_z(1, 1)
+    mirror(pair, 4, 6)
+    gather_relay_z(1, 2)
+    mirror(pair, 6, slots)
+    loop(3, nz, lambda dz: gather_relay_z(1, dz))
     own1 = product(pair, 0, NT)
     norm1 = sum_finish(2)
     beta = solve_t(norm0, norm1)

time: 59.6 us -> 62.3 us (1.045); the launches traced: 59.4 us -> 61.5 us
  Pallas kernels: 56.6 us -> 58.6 us
    pallas_call x1, Pallas kernels: 56.6 us -> 58.6 us  [body(): pl.pallas_call(functools.partial(kernel, n, ny), out_shape=jax.ShapeDtype...]
where the time goes in v3:
time: 62.3 us; the launch traced here: 61.5 us
  Pallas kernels  58.6 us (94%)
  local copies, waits for them, and re-layouts  1.53 us (2%)
  between operations  1.29 us (2%)
    pallas_call x1, Pallas kernels, body(): pl.pallas_call(functools.partial(kernel, n, ny), out_shape=jax.ShapeDtype...  58.6 us
    transpose x1, local copies, waits for them, and re-layouts, body(): return (out[0].T, out[1].T)  1.53 us

profile of v3, /device:TPU:0, one launch (start us, length us, event | category | flops | bytes accessed | tf_op | source)
XLA Modules:
  0.0 61.5 jit_solution(349755587171672622)
XLA Ops:
  1.3 58.6 %shard_map.59 = f32[2,32,512]{2,1,0:T(8,128)} custom-call(s32[1,8]{1,0:T(1,128)} %cols_ref.1, s32[1]{0:T(128)S(6)} %copy.6.count_ref, f32[32,512]{1,0:T(8,128)} %bitcast.9, f32[1,8,512,512]{3,2,1,0:T(8,128)} %blocks_ref.1), custom_call_target="tpu_custom_call" | custom-call | tf_op jit(solution)/shard_map/pallas_call | solution.py:421
  59.9 1.5 %slice_bitcast_fusion = (f32[512,32]{0,1:T(8,128)}, f32[512,32]{0,1:T(8,128)}) fusion(f32[2,32,512]{2,1,0:T(8,128)} %shard_map.59), kind=kLoop, calls=%fused_computation | loop fusion | bytes 262144 | tf_op jit(solution)/shard_map/transpose | solution.py:458
